TPU v7x, 32 devices: a whole 2x2x4 slice. The times are simulated.
32 devices in a mesh: groups: 2 (over x), ctx: 16 (over z, y, core).
Axes of the slice: x: 2, y: 2, z: 4, core: 2. Of those that a mesh axis runs over, the one named last changes fastest.
Arguments:
- queries: bfloat16 [8192, 1024], P(('groups', 'ctx')), parts along dimension 0, may hold values from -15 to 15
- key_rows: bfloat16 [8192, 1024], P(('groups', 'ctx')), parts along dimension 0, may hold values from -15 to 15
- value_rows: bfloat16 [8192, 1024], P(('groups', 'ctx')), parts along dimension 0, may hold values from -6 to 6
- out_grad: bfloat16 [8192, 2048], P(('groups', 'ctx')), parts along dimension 0, may hold values from -6 to 6
- out_weight: bfloat16 [2048, 1024], P('ctx'), may hold values from -0.1875 to 0.1875
- pair_allowed: int32 [64, 2], P('groups'), parts along dimension 0, may hold values 0 or 1
Outputs:
- layer_out: bfloat16 [8192, 2048], P(('groups', 'ctx')), parts along dimension 0
- query_grad: bfloat16 [8192, 1024], P(('groups', 'ctx')), parts along dimension 0
- key_grad: bfloat16 [8192, 1024], P(('groups', 'ctx')), parts along dimension 0
- value_grad: bfloat16 [8192, 1024], P(('groups', 'ctx')), parts along dimension 0
- weight_grad: float32 [4096, 1024], P(('groups', 'ctx')), parts along dimension 0
There are 2 independent parts, one for each index of `groups`. A program takes and returns all parts, laid end to end along the dimension named above; an argument that names none is the same for every part. Nothing has to cross between parts.
All inputs are finite; a program needn't handle non-finite values.
Results may differ from a plain program's by a relative error of at most 0.011.
Values may be sent and summed in bfloat16 or wider, within the bound.
A program may use at most 128 MiB of HBM per device.

v0:
```python
import math

import jax
import jax.numpy as jnp
from jax import lax
from jax.sharding import PartitionSpec as P

H = 8
HD = 128
BLK = 128
SPAN = 2


def shifted(block, axis, distance):
    devices = range(lax.axis_size(axis))
    route = [(i - distance, i) for i in devices if i - distance in devices]
    return lax.ppermute(block, axis, route)


def per_device(queries, key_rows, value_rows, out_grad, out_weight, pair_allowed):
    my_index = lax.axis_index("ctx")
    total_rows, feature_width = queries.shape
    count = total_rows // BLK
    inv_scale = 1.0 / math.sqrt(HD)
    own_keys = key_rows.reshape(count, BLK, feature_width)
    own_values = value_rows.reshape(count, BLK, feature_width)
    carried = shifted((own_keys, own_values), "ctx", 1)
    ext_keys = jnp.concatenate([carried[0], own_keys], axis=0)
    ext_values = jnp.concatenate([carried[1], own_values], axis=0)
    keys_sel = jnp.stack(
        [ext_keys[SPAN - shift_by : SPAN - shift_by + count] for shift_by in range(SPAN + 1)],
        axis=1,
    )
    values_sel = jnp.stack(
        [ext_values[SPAN - shift_by : SPAN - shift_by + count] for shift_by in range(SPAN + 1)],
        axis=1,
    )
    span_rows = (SPAN + 1) * BLK
    key_heads = keys_sel.reshape(count, span_rows, H, HD)
    value_heads = values_sel.reshape(count, span_rows, H, HD)
    query_heads = queries.reshape(count, BLK, H, HD)
    global_ids = my_index * count + jnp.arange(count, dtype=jnp.int32)
    allowed_rows = lax.dynamic_slice_in_dim(pair_allowed, my_index * count, count, 0)
    earlier = jnp.arange(1, SPAN + 1, dtype=jnp.int32)
    earlier_ok = (global_ids[:, None] - earlier[None, :] >= 0) & (allowed_rows > 0)
    valid = jnp.concatenate([jnp.ones((count, 1), bool), earlier_ok], axis=1)
    row_ids = jnp.arange(BLK, dtype=jnp.int32)
    col_ids = jnp.arange(span_rows, dtype=jnp.int32)
    col_block = col_ids // BLK
    diagonal = (col_ids[None, :] <= row_ids[:, None]) & (col_block[None, :] == 0)
    visible = diagonal[None] | valid[:, col_block][:, None, :] & (col_block[None, None, :] > 0)
    visible_heads = visible[:, None]
    scores = (
        jnp.einsum("aqhd,akhd->ahqk", query_heads, key_heads, preferred_element_type=jnp.float32)
        * inv_scale
    )
    safe = jnp.where(visible_heads, scores, -1e30)
    top_score = jnp.max(safe, axis=-1, keepdims=True)
    expo = jnp.where(visible_heads, jnp.exp(safe - top_score), 0.0)
    probs = expo / jnp.sum(expo, axis=-1, keepdims=True)
    probs_low = probs.astype(jnp.bfloat16)
    context = jnp.einsum(
        "ahqk,akhd->aqhd", probs_low, value_heads, preferred_element_type=jnp.float32
    )
    attn = context.astype(jnp.bfloat16).reshape(total_rows, feature_width)
    layer_full = lax.dot_general(
        attn,
        lax.all_gather(out_weight, "ctx", axis=0, tiled=True),
        (((1,), (1,)), ((), ())),
        preferred_element_type=jnp.float32,
    )
    columns = out_grad
    grad_full = jnp.dot(
        columns,
        lax.all_gather(out_weight, "ctx", axis=0, tiled=True),
        preferred_element_type=jnp.float32,
    )
    layer_out = layer_full.astype(jnp.bfloat16)
    attn_grad = grad_full.astype(jnp.bfloat16)
    columns = out_grad
    weight_grad = lax.psum_scatter(
        lax.dot_general(
            columns, attn, (((0,), (0,)), ((), ())), preferred_element_type=jnp.float32
        ),
        "ctx",
        scatter_dimension=0,
        tiled=True,
    )
    grad_heads = attn_grad.reshape(count, BLK, H, HD)
    prob_grad = jnp.einsum(
        "aqhd,akhd->ahqk", grad_heads, value_heads, preferred_element_type=jnp.float32
    )
    row_delta = jnp.einsum("aqhd,aqhd->ahq", grad_heads.astype(jnp.float32), context)
    score_grad = (probs * (prob_grad - row_delta[..., None]) * inv_scale).astype(jnp.bfloat16)
    query_part = jnp.einsum(
        "ahqk,akhd->aqhd", score_grad, key_heads, preferred_element_type=jnp.float32
    )
    query_grad = query_part.astype(jnp.bfloat16).reshape(total_rows, feature_width)
    key_part = jnp.einsum(
        "ahqk,aqhd->akhd", score_grad, query_heads, preferred_element_type=jnp.float32
    )
    value_part = jnp.einsum(
        "ahqk,aqhd->akhd", probs_low, grad_heads, preferred_element_type=jnp.float32
    )
    key_part = key_part.reshape(count, SPAN + 1, BLK, feature_width)
    value_part = value_part.reshape(count, SPAN + 1, BLK, feature_width)
    ext_key_grad = jnp.zeros((count + SPAN, BLK, feature_width), jnp.float32)
    ext_value_grad = jnp.zeros((count + SPAN, BLK, feature_width), jnp.float32)
    for shift_by in range(SPAN + 1):
        padding = ((SPAN - shift_by, shift_by), (0, 0), (0, 0))
        ext_key_grad = ext_key_grad + jnp.pad(key_part[:, shift_by], padding)
        ext_value_grad = ext_value_grad + jnp.pad(value_part[:, shift_by], padding)
    returned = (
        shifted(ext_key_grad[:SPAN].astype(jnp.bfloat16), "ctx", -1).astype(jnp.float32),
        shifted(ext_value_grad[:SPAN].astype(jnp.bfloat16), "ctx", -1).astype(jnp.float32),
    )
    own_key_grad = ext_key_grad[SPAN:] + returned[0]
    own_value_grad = ext_value_grad[SPAN:] + returned[1]
    key_grad = own_key_grad.reshape(total_rows, feature_width).astype(jnp.bfloat16)
    value_grad = own_value_grad.reshape(total_rows, feature_width).astype(jnp.bfloat16)
    return (layer_out, query_grad, key_grad, value_grad, weight_grad)


def solution(mesh):
    placed = (
        P(("groups", "ctx"), None),
        P(("groups", "ctx"), None),
        P(("groups", "ctx"), None),
        P(("groups", "ctx"), None),
        P("ctx", None),
        P("groups", None),
    )
    return jax.shard_map(
        per_device,
        mesh=mesh,
        in_specs=placed,
        out_specs=(
            P(("groups", "ctx"), None),
            P(("groups", "ctx"), None),
            P(("groups", "ctx"), None),
            P(("groups", "ctx"), None),
            P(("groups", "ctx"), None),
        ),
        check_vma=False,
    )
```

profile of v0, /device:TPU:8, one launch (start us, length us, event | category | flops | bytes accessed | tf_op | source)
XLA Modules:
  0.0 185.6 jit_solution(5070098945809545739)
XLA Ops:
  7.2 0.7 all-gather.2.cloned.1.call-update
  8.0 1.9 %collective-permute-start.1 = (bf16[2,128,1024]{2,1,0:T(8,128)(2,1)}, bf16[2,128,1024]{2,1,0:T(8,128)(2,1)S(1)}, u32[]{:S(2)}, u32[]{:S(2)}) collective-permute-start(bf16[2,128,1024]{2,1,0:T(8,128)(2,1)} %bitcast.120), channel_id=1, source_target_pairs={{0,1},{1,2},{2,3},{3,4},{4,5},{5,6},{6,7},{7,8},{8,9},{9,10},{10,1... | collective-permute-start | bytes 1572872 | tf_op jit(solution)/shard_map/ppermute | solution.py:17
  9.9 3.5 %collective-permute-start = (bf16[2,128,1024]{2,1,0:T(8,128)(2,1)}, bf16[2,128,1024]{2,1,0:T(8,128)(2,1)}, u32[]{:S(2)}, u32[]{:S(2)}) collective-permute-start(bf16[2,128,1024]{2,1,0:T(8,128)(2,1)} %bitcast.123), channel_id=1, source_target_pairs={{0,1},{1,2},{2,3},{3,4},{4,5},{5,6},{6,7},{7,8},{8,9},{9,10},{10,1... | collective-permute-start | bytes 1572872 | tf_op jit(solution)/shard_map/ppermute | solution.py:17
  13.5 0.8 compare_and_fusion
  14.3 1.3 gather_fusion
  15.8 1.1 copy.71
  17.3 2.3 %collective-permute-done.1 = bf16[2,128,1024]{2,1,0:T(8,128)(2,1)S(1)} collective-permute-done((bf16[2,128,1024]{2,1,0:T(8,128)(2,1)}, bf16[2,128,1024]{2,1,0:T(8,128)(2,1)S(1)}, u32[]{:S(2)}, u32[]{:S(2)}) %collective-permute-start.1) | collective-permute-done | bytes 524320 | tf_op jit(solution)/shard_map/ppermute | solution.py:17
  19.6 1.0 fusion.16
  20.8 1.6 copy.70
  22.4 2.1 %copy.42 = bf16[2,384,8,128]{1,3,2,0:T(8,128)(2,1)S(1)} copy(bf16[2,384,8,128]{3,2,1,0:T(8,128)(2,1)} %bitcast.112) | data formatting | bytes 3145728 | tf_op jit(solution)/shard_map/reshape | solution.py:39
  24.5 6.7 %collective-permute-done = bf16[2,128,1024]{2,1,0:T(8,128)(2,1)} collective-permute-done((bf16[2,128,1024]{2,1,0:T(8,128)(2,1)}, bf16[2,128,1024]{2,1,0:T(8,128)(2,1)}, u32[]{:S(2)}, u32[]{:S(2)}) %collective-permute-start) | collective-permute-done | bytes 524320 | tf_op jit(solution)/shard_map/ppermute | solution.py:17
  31.2 1.1 fusion.17
  32.3 1.4 pad_maximum_fusion
  33.8 0.4 copy.69
  34.3 0.6 fusion.21
  34.9 1.3 fusion.34
  36.2 2.2 %bitcast_convert_fusion = (bf16[2,128,8,128]{1,3,2,0:T(8,128)(2,1)}, f32[2,8,128,128]{3,2,1,0:T(8,128)}) fusion(f32[2,8,128,384]{2,3,1,0:T(8,128)S(1)} %get-tuple-element.22, f32[2,8,128]{2,1,0:T(8,128)S(1)} %get-tuple-element.21, bf16[2,384,8,128]{3,2,1,0:T(8,128)(2,1)S(1)} %bitcast.128), kind=kOutput, calls=%fused_computation.40 | convolution fusion | flops 203161600 | bytes 6299648 | tf_op jit(solution)/shard_map/ahqk,akhd->aqhd/dot_general | solution.py:62
  38.4 2.1 %copy.38 = bf16[2,128,8,128]{3,2,1,0:T(8,128)(2,1)} copy(bf16[2,128,8,128]{1,3,2,0:T(8,128)(2,1)} %get-tuple-element.23) | data formatting | bytes 1048576 | tf_op jit(solution)/shard_map/convert_element_type | solution.py:65
  40.5 5.6 %convolution_bitcast_fusion = f32[2048,1024]{0,1:T(8,128)} fusion(bf16[256,2048]{1,0:T(8,128)(2,1)S(1)} %copy-done, bf16[32,8,8,128]{3,2,1,0:T(8,128)(2,1)} %bitcast.118), kind=kOutput, calls=%fused_computation.2 | convolution fusion | flops 1073741824 | bytes 9961472 | tf_op jit(solution)/shard_map/dot_general | solution.py:82
  46.1 17.3 %all-gather.2.cloned.1.call-done = bf16[2048,1024]{1,0:T(8,128)(2,1)} async-done(((bf16[128,1024]{1,0:T(8,128)(2,1)}), bf16[2048,1024]{1,0:T(8,128)(2,1)}) %all-gather.2.cloned.1.call-update) | async-done | bytes 4194320 | tf_op jit(solution)/shard_map/all_gather | solution.py:68
  63.4 3.4 %fusion.9 = bf16[32,8,8,128]{3,1,2,0:T(8,128)(2,1)S(1)} fusion(bf16[256,2048]{1,0:T(8,128)(2,1)S(1)} %copy-done, bf16[2048,1024]{1,0:T(8,128)(2,1)} %all-gather.2.cloned.1.call-done), kind=kOutput, calls=%fused_computation.24 | convolution fusion | flops 1074003968 | bytes 5767168 | tf_op jit(solution)/shard_map/dot_general | solution.py:73
  67.0 1.1 copy.49
  68.1 1.1 bitcast_convert_fusion.1
  69.1 1.6 copy.62
  70.7 1.8 fusion.13
  72.9 3.1 %multiply_convert_fusion = bf16[2,8,128,384]{2,3,1,0:T(8,128)(2,1)S(1)} fusion(bf16[2,128,8,128]{1,3,2,0:T(8,128)(2,1)S(1)} %copy-done.10, f32[2,8,128]{2,1,0:T(8,128)S(1)} %fusion.13, bf16[2,384,8,128]{3,2,1,0:T(8,128)(2,1)S(1)} %bitcast.129, f32[2,8,128,384]{2,3,1,0:T(8,128)} %copy-done.13, f32[2,8,128]{2,1,0:T(8,128)S(1)} %get-tuple-element.21), kind=kOutput, calls=%fused_computation.4 | convolution fusion | flops 205258752 | bytes 6832128 | tf_op jit(solution)/shard_map/aqhd,akhd->ahqk/dot_general | solution.py:90
  76.0 1.1 copy-done.4
  77.1 1.4 fusion.10
  78.5 1.5 copy.44
  80.1 0.9 copy.94
  81.0 0.6 convolution_bitcast_fusion.2
  81.5 3.5 %copy.46 = f32[2,384,8,128]{3,2,1,0:T(8,128)} copy(f32[2,384,8,128]{3,1,2,0:T(8,128)S(1)} %convolution_bitcast_fusion.2) | data formatting | bytes 6291456 | tf_op jit(solution)/shard_map/ahqk,aqhd->akhd/transpose | solution.py:99
  85.0 3.1 %reshape.182 = f32[2,3,128,1024]{3,2,1,0:T(8,128)S(1)} reshape(f32[2,384,8,128]{3,2,1,0:T(8,128)} %copy.46) | data formatting | bytes 6291456 | tf_op jit(solution)/shard_map/reshape | solution.py:105
  88.1 0.4 slice_bitcast_fusion.5
  88.9 1.3 copy-done.2
  90.2 0.9 slice.77
  91.1 1.9 %collective-permute-start.2 = (bf16[2,128,1024]{2,1,0:T(8,128)(2,1)}, bf16[2,128,1024]{2,1,0:T(8,128)(2,1)}, u32[]{:S(2)}, u32[]{:S(2)}) collective-permute-start(bf16[2,128,1024]{2,1,0:T(8,128)(2,1)} %slice.77), channel_id=1, source_target_pairs={{1,0},{2,1},{3,2},{4,3},{5,4},{6,5},{7,6},{8,7},{9,8},{10,9},{11,1... | collective-permute-start | bytes 1572872 | tf_op jit(solution)/shard_map/ppermute | solution.py:17
  93.0 0.8 convolution_bitcast_fusion.1
  93.8 2.4 %copy.51 = f32[2,384,8,128]{3,2,1,0:T(8,128)} copy(f32[2,384,8,128]{1,3,2,0:T(8,128)S(1)} %convolution_bitcast_fusion.1) | data formatting | bytes 6291456 | tf_op jit(solution)/shard_map/ahqk,aqhd->akhd/transpose | solution.py:102
  96.1 3.1 %reshape.183 = f32[2,3,128,1024]{3,2,1,0:T(8,128)S(1)} reshape(f32[2,384,8,128]{3,2,1,0:T(8,128)} %copy.51) | data formatting | bytes 6291456 | tf_op jit(solution)/shard_map/reshape | solution.py:106
  100.1 2.3 %collective-permute-start.3 = (bf16[2,128,1024]{2,1,0:T(8,128)(2,1)S(1)}, bf16[2,128,1024]{2,1,0:T(8,128)(2,1)S(1)}, u32[]{:S(2)}, u32[]{:S(2)}) collective-permute-start(bf16[2,128,1024]{2,1,0:T(8,128)(2,1)S(1)} %slice.76), channel_id=1, source_target_pairs={{1,0},{2,1},{3,2},{4,3},{5,4},{6,5},{7,6},{8,7},{9,8},{10,9},{11,1... | collective-permute-start | bytes 1572872 | tf_op jit(solution)/shard_map/ppermute | solution.py:17
  102.4 2.3 %convolution_convert_fusion = bf16[256,2048]{1,0:T(8,128)(2,1)} fusion(bf16[2048,1024]{1,0:T(8,128)(2,1)S(1)} %copy-done.12, bf16[32,8,8,128]{3,2,1,0:T(8,128)(2,1)S(1)} %bitcast.119), kind=kOutput, calls=%fused_computation.6 | convolution fusion | flops 1074266112 | bytes 5767168 | tf_op jit(solution)/shard_map/dot_general | solution.py:66
  104.7 3.3 %collective-permute-done.2 = bf16[2,128,1024]{2,1,0:T(8,128)(2,1)} collective-permute-done((bf16[2,128,1024]{2,1,0:T(8,128)(2,1)}, bf16[2,128,1024]{2,1,0:T(8,128)(2,1)}, u32[]{:S(2)}, u32[]{:S(2)}) %collective-permute-start.2) | collective-permute-done | bytes 524320 | tf_op jit(solution)/shard_map/ppermute | solution.py:17
  108.0 2.1 %fusion.12 = bf16[2,128,1024]{2,1,0:T(8,128)(2,1)} fusion(f32[4,128,1024]{2,1,0:T(8,128)S(1)} %copy-done.3, bf16[2,128,1024]{2,1,0:T(8,128)(2,1)} %collective-permute-done.2), kind=kLoop, calls=%fused_computation.34 | loop fusion | flops 786432 | bytes 2097152 | tf_op jit(solution)/shard_map/convert_element_type | solution.py:119
  110.1 25.3 %collective-permute-done.3 = bf16[2,128,1024]{2,1,0:T(8,128)(2,1)S(1)} collective-permute-done((bf16[2,128,1024]{2,1,0:T(8,128)(2,1)S(1)}, bf16[2,128,1024]{2,1,0:T(8,128)(2,1)S(1)}, u32[]{:S(2)}, u32[]{:S(2)}) %collective-permute-start.3) | collective-permute-done | bytes 524320 | tf_op jit(solution)/shard_map/ppermute | solution.py:17
  135.4 0.9 fusion.11
  136.3 40.4 %reduce-scatter.2.cloned.1.call-done = f32[128,1024]{0,1:T(8,128)} async-done(((f32[2048,1024]{0,1:T(8,128)}), f32[128,1024]{0,1:T(8,128)}) %reduce-scatter.2.cloned.1.call-update) | async-done | bytes 524304 | tf_op jit(solution)/shard_map/reduce_scatter | solution.py:81
  176.7 2.0 %copy.54 = f32[128,1024]{1,0:T(8,128)} copy(f32[128,1024]{0,1:T(8,128)} %reduce-scatter.2.cloned.1.call-done) | data formatting | bytes 1048576
  (48 shorter events, 2.7 us)
Async XLA Ops:
  7.2 33.3 %copy-start = (bf16[256,2048]{1,0:T(8,128)(2,1)S(1)}, bf16[256,2048]{1,0:T(8,128)(2,1)}, u32[]{:S(2)}) copy-start(bf16[256,2048]{1,0:T(8,128)(2,1)} %param.9) | copy-start | bytes 3145732
  7.2 13.4 %copy-start.7 = (bf16[256,1024]{1,0:T(8,128)(2,1)S(1)}, bf16[256,1024]{1,0:T(8,128)(2,1)}, u32[]{:S(2)}) copy-start(bf16[256,1024]{1,0:T(8,128)(2,1)} %param.7) | copy-start | bytes 1572868
  7.2 56.2 %all-gather.2.cloned.1.call-start = ((), (), s32[]{:S(2)}) async-start(), calls=%async_computation.1 | async-start | bytes 4456448 | tf_op jit(solution)/shard_map/all_gather | solution.py:68
  7.9 168.8 %reduce-scatter.2.cloned.1.call-start = ((), (), s32[]{:S(2)}) async-start(), calls=%async_computation.2 | async-start | bytes 8912896 | tf_op jit(solution)/shard_map/reduce_scatter | solution.py:81
  8.0 11.6 %collective-permute-start.1 = (bf16[2,128,1024]{2,1,0:T(8,128)(2,1)}, bf16[2,128,1024]{2,1,0:T(8,128)(2,1)S(1)}, u32[]{:S(2)}, u32[]{:S(2)}) collective-permute-start(bf16[2,128,1024]{2,1,0:T(8,128)(2,1)} %bitcast.120), channel_id=1, source_target_pairs={{0,1},{1,2},{2,3},{3,4},{4,5},{5,6},{6,7},{7,8},{8,9},{9,10},{10,1... | collective-permute-start | bytes 1572872 | tf_op jit(solution)/shard_map/ppermute | solution.py:17
  9.9 21.3 %collective-permute-start = (bf16[2,128,1024]{2,1,0:T(8,128)(2,1)}, bf16[2,128,1024]{2,1,0:T(8,128)(2,1)}, u32[]{:S(2)}, u32[]{:S(2)}) collective-permute-start(bf16[2,128,1024]{2,1,0:T(8,128)(2,1)} %bitcast.123), channel_id=1, source_target_pairs={{0,1},{1,2},{2,3},{3,4},{4,5},{5,6},{6,7},{7,8},{8,9},{9,10},{10,1... | collective-permute-start | bytes 1572872 | tf_op jit(solution)/shard_map/ppermute | solution.py:17
  34.3 1.9 %copy-start.8 = (bf16[96,8,8,128]{3,2,1,0:T(8,128)(2,1)}, bf16[96,8,8,128]{3,2,1,0:T(8,128)(2,1)S(1)}, u32[]{:S(2)}) copy-start(bf16[96,8,8,128]{3,2,1,0:T(8,128)(2,1)S(1)} %copy.69) | copy-start | bytes 4718596
  36.2 2.2 %copy-start.13 = (f32[2,8,128,384]{2,3,1,0:T(8,128)}, f32[2,8,128,384]{2,3,1,0:T(8,128)S(1)}, u32[]{:S(2)}) copy-start(f32[2,8,128,384]{2,3,1,0:T(8,128)S(1)} %get-tuple-element.22) | copy-start | bytes 9437188
  70.7 2.1 %copy-start.9 = (bf16[96,8,8,128]{3,2,1,0:T(8,128)(2,1)S(1)}, bf16[96,8,8,128]{3,2,1,0:T(8,128)(2,1)}, u32[]{:S(2)}) copy-start(bf16[96,8,8,128]{3,2,1,0:T(8,128)(2,1)} %copy-done.8) | copy-start | bytes 4718596
  70.7 2.2 %copy-start.10 = (bf16[2,128,8,128]{1,3,2,0:T(8,128)(2,1)S(1)}, bf16[2,128,8,128]{1,3,2,0:T(8,128)(2,1)}, u32[]{:S(2)}) copy-start(bf16[2,128,8,128]{1,3,2,0:T(8,128)(2,1)} %copy.49) | copy-start | bytes 1572868
  76.0 1.1 copy-start.4
  78.5 2.4 %copy-start.5 = (bf16[2,8,128,384]{2,3,1,0:T(8,128)(2,1)S(1)}, bf16[2,8,128,384]{2,3,1,0:T(8,128)(2,1)}, u32[]{:S(2)}) copy-start(bf16[2,8,128,384]{2,3,1,0:T(8,128)(2,1)} %copy-done.4) | copy-start | bytes 4718596
  88.5 4.5 %copy-start.11 = (bf16[2,128,8,128]{1,3,2,0:T(8,128)(2,1)S(1)}, bf16[2,128,8,128]{1,3,2,0:T(8,128)(2,1)}, u32[]{:S(2)}) copy-start(bf16[2,128,8,128]{1,3,2,0:T(8,128)(2,1)} %copy.49) | copy-start | bytes 1572868
  88.5 4.5 %copy-start.14 = (f32[2,8,128,384]{2,3,1,0:T(8,128)S(1)}, f32[2,8,128,384]{2,3,1,0:T(8,128)}, u32[]{:S(2)}) copy-start(f32[2,8,128,384]{2,3,1,0:T(8,128)} %copy-done.13) | copy-start | bytes 9437188
  88.9 1.3 copy-start.2
  91.1 16.9 %collective-permute-start.2 = (bf16[2,128,1024]{2,1,0:T(8,128)(2,1)}, bf16[2,128,1024]{2,1,0:T(8,128)(2,1)}, u32[]{:S(2)}, u32[]{:S(2)}) collective-permute-start(bf16[2,128,1024]{2,1,0:T(8,128)(2,1)} %slice.77), channel_id=1, source_target_pairs={{1,0},{2,1},{3,2},{4,3},{5,4},{6,5},{7,6},{8,7},{9,8},{10,9},{11,1... | collective-permute-start | bytes 1572872 | tf_op jit(solution)/shard_map/ppermute | solution.py:17
  99.7 2.7 %copy-start.6 = (bf16[2,128,8,128]{3,2,1,0:T(8,128)(2,1)S(1)}, bf16[2,128,8,128]{3,2,1,0:T(8,128)(2,1)}, u32[]{:S(2)}) copy-start(bf16[2,128,8,128]{3,2,1,0:T(8,128)(2,1)} %copy.38) | copy-start | bytes 1572868
  99.7 2.7 %copy-start.12 = (bf16[2048,1024]{1,0:T(8,128)(2,1)S(1)}, bf16[2048,1024]{1,0:T(8,128)(2,1)}, u32[]{:S(2)}) copy-start(bf16[2048,1024]{1,0:T(8,128)(2,1)} %all-gather.2.cloned.1.call-done) | copy-start | bytes 12582916
  100.1 7.9 %copy-start.3 = (f32[4,128,1024]{2,1,0:T(8,128)S(1)}, f32[4,128,1024]{2,1,0:T(8,128)}, u32[]{:S(2)}) copy-start(f32[4,128,1024]{2,1,0:T(8,128)} %copy-done.2) | copy-start | bytes 6291460
  100.1 35.3 %collective-permute-start.3 = (bf16[2,128,1024]{2,1,0:T(8,128)(2,1)S(1)}, bf16[2,128,1024]{2,1,0:T(8,128)(2,1)S(1)}, u32[]{:S(2)}, u32[]{:S(2)}) collective-permute-start(bf16[2,128,1024]{2,1,0:T(8,128)(2,1)S(1)} %slice.76), channel_id=1, source_target_pairs={{1,0},{2,1},{3,2},{4,3},{5,4},{6,5},{7,6},{8,7},{9,8},{10,9},{11,1... | collective-permute-start | bytes 1572872 | tf_op jit(solution)/shard_map/ppermute | solution.py:17
  108.0 70.7 %copy-start.1 = (bf16[256,2048]{1,0:T(8,128)(2,1)S(1)}, bf16[256,2048]{1,0:T(8,128)(2,1)}, u32[]{:S(2)}) copy-start(bf16[256,2048]{1,0:T(8,128)(2,1)} %param.9) | copy-start | bytes 3145732
Sparse Core Ops, SparseCore 0:
  10.2 53.1 all-gather.1
  67.5 109.1 reduce-scatter.1
where the time goes:
time: 188 us; the launch traced here: 186 us
  waiting for transfers between devices  96 us (51%)
  local copies, waits for them, and re-layouts  32.9 us (18%)
  matrix products  19.9 us (11%)
  between operations  14.4 us (8%)
  other arithmetic  12.7 us (7%)
  starting transfers between devices  9.76 us (5%)
    reduce_scatter x1, waiting for transfers between devices, per_device(): lax.psum_scatter(lax.dot_general(columns, attn, (((0,), (0,)), ((), ())),...  40.4 us
    ppermute x4, waiting for transfers between devices, shifted(): return lax.ppermute(block, axis, route)  37.6 us
    all_gather x1, waiting for transfers between devices, per_device(): lax.all_gather(out_weight, 'ctx', axis=0, tiled=True)  17.3 us
    unnamed x37, local copies, waits for them, and re-layouts  10.6 us
    ppermute x4, starting transfers between devices, shifted(): return lax.ppermute(block, axis, route)  9.68 us
    dot_general x1, matrix products, per_device(): lax.dot_general(columns, attn, (((0,), (0,)), ((), ())), preferred_elemen...  5.55 us
  transfers between devices with their start and end apart: 6, of which 6 were waited for; matrix products, arithmetic and copies ran while one was open for 33% of the time, Pallas kernels for 0%

commit v1 on v0

v1 whole, which is shorter than its diff:
```python
import functools
import math

import jax
import jax.numpy as jnp
from jax import lax
from jax.experimental import pallas as pl
from jax.experimental.pallas import tpu as pltpu
from jax.sharding import PartitionSpec as P

H = 8
HD = 128
BLK = 128
SPAN = 2
CHUNK = 256
MESH = pl.DeviceIdType.MESH
F32 = jnp.float32
BF16 = jnp.bfloat16
NEG = -1e30


def dot(a, b, ca, cb):
    return lax.dot_general(a, b, (((ca,), (cb,)), ((), ())), preferred_element_type=F32)


def kernel(
    n,
    pa, q, k, v, og, w,
    lo, qg, kg, vg, wg,
    wbuf, part, from_core, y_out, y_in, z_out, z_in,
    k_halo, v_halo, dk_out, dv_out, dk_in, dv_in, dk_own, dv_own,
    probs_buf, ctx_buf, attn, da, bias,
    w_send, w_recv, halo_send, halo_recv, back_send, back_recv,
    c_send, c_recv, y_send, y_recv, z_send, z_recv,
):
    g = lax.axis_index("groups")
    me = lax.axis_index("ctx")
    zs = n // 4
    rows = q.shape[0]
    half = q.shape[1] // 2
    depth = w.shape[0]
    per_chunk = CHUNK // depth
    chunks = og.shape[1] // CHUNK
    core = lax.rem(me, 2)
    chip = me // 2
    y = lax.rem(chip, 2)
    z = chip // 2
    hm = lax.rem(g, 2)
    ho = 1 - hm
    inv_scale = 1.0 / math.sqrt(HD)

    def index(zz, yy, cc):
        return (zz * 2 + yy) * 2 + cc

    sib = (g, index(z, y, 1 - core))
    ypeer = (g, index(z, 1 - y, core))
    xpeer = (g + 1 - 2 * hm, me)
    up = (g, lax.rem(me + 1, n))
    down = (g, lax.rem(me + n - 1, n))

    def rc(src, dst, ss, rs, dev):
        return pltpu.make_async_remote_copy(
            src_ref=src, dst_ref=dst, send_sem=ss, recv_sem=rs,
            device_id=dev, device_id_type=MESH,
        )

    barrier = pltpu.get_barrier_semaphore()
    for dev in (sib, ypeer, xpeer, up, down):
        pl.semaphore_signal(barrier, inc=1, device_id=dev, device_id_type=MESH)
    for step in range(1, zs):
        dev = (g, index(lax.rem(z + step, zs), y, core))
        pl.semaphore_signal(barrier, inc=1, device_id=dev, device_id_type=MESH)

    wbuf[0, me] = w[:, :half]
    wbuf[1, me] = w[:, half:]
    pl.semaphore_wait(barrier, 5 + zs - 1)

    def halo(i, part_of):
        src, dst = ((k, k_halo), (v, v_halo))[part_of]
        return rc(src.at[:, pl.ds(i * half, half)], dst.at[i],
                  halo_send.at[2 * i + part_of], halo_recv.at[2 * i + part_of], up)

    @pl.when(me < n - 1)
    def _():
        for i in range(2):
            for part_of in range(2):
                halo(i, part_of).start()

    def w_copy(kind, h, idx, dev):
        return rc(wbuf.at[h, idx], wbuf.at[h, idx], w_send.at[kind, h, idx], w_recv.at[h, idx], dev)

    def z_own(step):
        dev = (g, index(lax.rem(z + step, zs), y, core))
        return rc(wbuf.at[hm, me], wbuf.at[hm, me], w_send.at[3, 0, step], w_recv.at[hm, me], dev)

    def start_z(step, c):
        z_own(step).start()
        return c

    lax.fori_loop(1, zs, start_z, 0)
    w_copy(0, hm, me, ypeer).start()
    w_copy(2, 0, me, sib).start()
    w_copy(2, 1, me, sib).start()

    row_ids = lax.broadcasted_iota(jnp.int32, (BLK, BLK), 0)
    col_ids = lax.broadcasted_iota(jnp.int32, (BLK, BLK), 1)
    count = rows // BLK
    for a in range(count):
        blk = me * count + a
        for e in range(count + SPAN):
            back = a + SPAN - e
            if back == 0:
                tile = jnp.where(col_ids <= row_ids, 0.0, NEG)
            elif 0 < back <= SPAN:
                ok = pa[blk, back - 1] * jnp.where(blk >= back, 1, 0)
                tile = jnp.where(jnp.full((BLK, BLK), ok, jnp.int32) > 0, 0.0, NEG)
            else:
                tile = jnp.full((BLK, BLK), NEG, F32)
            bias[a * BLK:(a + 1) * BLK, e * BLK:(e + 1) * BLK] = tile

    def from_z(step, c):
        idx = index(lax.rem(z + step, zs), y, core)
        w_copy(0, hm, idx, ypeer).wait_recv()
        w_copy(0, hm, idx, ypeer).start()
        w_copy(1, hm, idx, xpeer).start()
        w_copy(2, hm, idx, sib).start()
        return c

    lax.fori_loop(1, zs, from_z, 0)

    @pl.when(me == 0)
    def _():
        k_halo[...] = jnp.zeros_like(k_halo)
        v_halo[...] = jnp.zeros_like(v_halo)

    def ext(ref, halo_ref, i, j):
        at = pl.ds(pl.multiple_of(j * HD, HD), HD)
        own = pl.ds(pl.multiple_of(i * half + j * HD, HD), HD)
        return jnp.concatenate([halo_ref[i, :, at], ref[:, own]], axis=0), own

    for i in range(2):
        @pl.when(me > 0)
        def _():
            for part_of in range(2):
                halo(i, part_of).wait_recv()

        def forward(j, c):
            keys, own = ext(k, k_halo, i, j)
            values, _ = ext(v, v_halo, i, j)
            s = dot(q[:, own], keys, 1, 1) * inv_scale + bias[...]
            e = jnp.exp(s - jnp.max(s, axis=-1, keepdims=True))
            probs = e * (1.0 / jnp.sum(e, axis=-1, keepdims=True))
            probs_buf[i * (H // 2) + j] = probs
            context = dot(probs.astype(BF16), values, 1, 0)
            ctx_buf[:, own] = context
            attn[:, own] = context.astype(BF16)
            return c

        lax.fori_loop(0, H // 2, forward, 0)

    def c_copy(o):
        return rc(part.at[o * 2 + 1 - core], from_core.at[o], c_send.at[o], c_recv.at[o], sib)

    def share(t, c):
        j = lax.rem(t + 1 + (z * 2 * depth * 2) // CHUNK, chunks)
        cols = pl.ds(pl.multiple_of(j * CHUNK, CHUNK), CHUNK)
        r = dot(og[:, cols], attn[...], 0, 0).astype(BF16)
        part[pl.ds(j * per_chunk, per_chunk)] = r.reshape(per_chunk, depth, 2 * half)
        for b in range(per_chunk // 2):
            c_copy(j * (per_chunk // 2) + b).start()
        return c

    lax.fori_loop(0, chunks, share, 0)

    def y_copy(zz):
        return rc(y_out.at[zz], y_in.at[zz], y_send.at[zz], y_recv.at[zz], ypeer)

    def stage_y(step, c):
        zz = lax.rem(z + step, zs)
        o = zz * 2 + 1 - y
        c_copy(o).wait_recv()
        y_out[zz] = (part[o * 2 + core].astype(F32) + from_core[o].astype(F32)).astype(BF16)
        y_copy(zz).start()
        return c

    lax.fori_loop(1, zs + 1, stage_y, 0)

    def from_y(step, c):
        idx = index(lax.rem(z + step, zs), 1 - y, core)
        w_copy(0, hm, idx, xpeer).wait_recv()
        w_copy(1, hm, idx, xpeer).start()
        w_copy(2, hm, idx, sib).start()
        return c

    lax.fori_loop(0, zs, from_y, 0)

    def from_x(step, c):
        for yy in range(2):
            idx = index(lax.rem(z + step, zs), (y, 1 - y)[yy], core)

            def go(idx=idx):
                w_copy(1, ho, idx, xpeer).wait_recv()
                w_copy(2, ho, idx, sib).start()

            if yy == 0:
                pl.when(step > 0)(go)
            else:
                go()
        return c

    lax.fori_loop(0, zs, from_x, 0)

    def from_sib(o, c):
        for h in range(2):
            w_copy(2, h, o * 2 + 1 - core, sib).wait_recv()
        return c

    lax.fori_loop(0, n // 2, from_sib, 0)

    for h in range(2):
        for part_of in range(half // CHUNK):
            cols = slice(part_of * CHUNK, (part_of + 1) * CHUNK)
            r = dot(og[...], wbuf[h, :, :, cols].reshape(n * depth, CHUNK), 1, 0)
            da[:, h * half + part_of * CHUNK:h * half + (part_of + 1) * CHUNK] = r.astype(BF16)

    def back_copy(i, part_of):
        src, dst = ((dk_out, dk_in), (dv_out, dv_in))[part_of]
        at = 2 * i + part_of
        return rc(src.at[i], dst.at[i], back_send.at[at], back_recv.at[at], down)

    for i in range(2):
        def backward(j, c):
            keys, own = ext(k, k_halo, i, j)
            values, _ = ext(v, v_halo, i, j)
            at = pl.ds(pl.multiple_of(j * HD, HD), HD)
            d = da[:, own]
            probs = probs_buf[i * (H // 2) + j]
            delta = jnp.sum(d.astype(F32) * ctx_buf[:, own], axis=-1, keepdims=True)
            sg = (probs * (dot(d, values, 1, 1) - delta) * inv_scale).astype(BF16)
            dk = dot(sg, q[:, own], 0, 0)
            dv = dot(probs.astype(BF16), d, 0, 0)
            dk_out[i, :, at] = dk[:rows].astype(BF16)
            dv_out[i, :, at] = dv[:rows].astype(BF16)
            dk_own[:, own] = dk[rows:]
            dv_own[:, own] = dv[rows:]
            qg[:, own] = dot(sg, keys, 1, 0).astype(BF16)
            return c

        lax.fori_loop(0, H // 2, backward, 0)

        @pl.when(me > 0)
        def _():
            for part_of in range(2):
                back_copy(i, part_of).start()

    def z_copy(zz, slot):
        return rc(z_out.at[zz], z_in.at[slot], z_send.at[zz], z_recv.at[slot], (g, index(zz, y, core)))

    def summed(zz):
        o = zz * 2 + y
        c_copy(o).wait_recv()
        y_copy(zz).wait_recv()
        return part[o * 2 + core].astype(F32) + from_core[o].astype(F32) + y_in[zz].astype(F32)

    def stage_z(step, c):
        zz = lax.rem(z + step, zs)
        z_out[zz] = summed(zz).astype(BF16)
        z_copy(zz, z).start()
        return c

    lax.fori_loop(1, zs, stage_z, 0)

    def layer(j, c):
        rows_of = pl.ds(j * per_chunk, per_chunk)
        r = dot(attn[:, :half], wbuf[0, rows_of].reshape(CHUNK, half), 1, 1)
        r = r + dot(attn[:, half:], wbuf[1, rows_of].reshape(CHUNK, half), 1, 1)
        lo[:, pl.ds(pl.multiple_of(j * CHUNK, CHUNK), CHUNK)] = r.astype(BF16)
        return c

    lax.fori_loop(0, chunks, layer, 0)

    wg[...] = summed(z)

    for i in range(2):
        cols = slice(i * half, (i + 1) * half)

        @pl.when(me < n - 1)
        def _():
            for part_of in range(2):
                back_copy(i, part_of).wait_recv()
            kg[:, cols] = (dk_own[:, cols] + dk_in[i].astype(F32)).astype(BF16)
            vg[:, cols] = (dv_own[:, cols] + dv_in[i].astype(F32)).astype(BF16)

        @pl.when(me == n - 1)
        def _():
            kg[:, cols] = dk_own[:, cols].astype(BF16)
            vg[:, cols] = dv_own[:, cols].astype(BF16)

    def last(step, c):
        zz = lax.rem(z + step, zs)
        z_copy(zz, zz).wait_recv()
        wg[...] += z_in[zz].astype(F32)
        return c

    lax.fori_loop(1, zs, last, 0)

    @pl.when(me < n - 1)
    def _():
        for i in range(2):
            for part_of in range(2):
                halo(i, part_of).wait_send()

    @pl.when(me > 0)
    def _():
        for i in range(2):
            for part_of in range(2):
                back_copy(i, part_of).wait_send()

    def sent(step, c):
        zz = lax.rem(z + step, zs)
        mine = index(zz, y, core)
        other = index(zz, 1 - y, core)
        w_copy(0, hm, mine, ypeer).wait_send()
        w_copy(1, hm, other, xpeer).wait_send()
        w_copy(2, hm, mine, sib).wait_send()
        w_copy(2, ho, mine, sib).wait_send()
        w_copy(2, hm, other, sib).wait_send()
        w_copy(2, ho, other, sib).wait_send()
        y_copy(zz).wait_send()
        c_copy(zz * 2).wait_send()
        c_copy(zz * 2 + 1).wait_send()

        @pl.when(step > 0)
        def _():
            z_own(step).wait_send()
            w_copy(1, hm, mine, xpeer).wait_send()
            z_copy(zz, z).wait_send()

        return c

    lax.fori_loop(0, zs, sent, 0)


def per_device(n, queries, key_rows, value_rows, out_grad, out_weight, pair_allowed):
    rows, width = queries.shape
    model = out_grad.shape[1]
    depth = out_weight.shape[0]
    zs = n // 4
    half = width // 2
    vmem = pl.BlockSpec(memory_space=pltpu.VMEM)
    dma = pltpu.SemaphoreType.DMA
    return pl.pallas_call(
        functools.partial(kernel, n),
        out_shape=(
            jax.ShapeDtypeStruct((rows, model), BF16),
            jax.ShapeDtypeStruct((rows, width), BF16),
            jax.ShapeDtypeStruct((rows, width), BF16),
            jax.ShapeDtypeStruct((rows, width), BF16),
            jax.ShapeDtypeStruct((depth, width), F32),
        ),
        in_specs=[pl.BlockSpec(memory_space=pltpu.SMEM)] + [vmem] * 5,
        out_specs=(vmem,) * 5,
        scratch_shapes=[
            pltpu.VMEM((2, n, depth, half), BF16),
            pltpu.VMEM((n, depth, width), BF16),
            pltpu.VMEM((n // 2, depth, width), BF16),
            pltpu.VMEM((zs, depth, width), BF16),
            pltpu.VMEM((zs, depth, width), BF16),
            pltpu.VMEM((zs, depth, width), BF16),
            pltpu.VMEM((zs, depth, width), BF16),
        ]
        + [pltpu.VMEM((2, rows, half), BF16)] * 6
        + [
            pltpu.VMEM((rows, width), F32),
            pltpu.VMEM((rows, width), F32),
            pltpu.VMEM((H, rows, rows + SPAN * BLK), F32),
            pltpu.VMEM((rows, width), F32),
            pltpu.VMEM((rows, width), BF16),
            pltpu.VMEM((rows, width), BF16),
            pltpu.VMEM((rows, rows + SPAN * BLK), F32),
            dma((4, 2, n)),
            dma((2, n)),
            dma((4,)), dma((4,)), dma((4,)), dma((4,)),
            dma((n // 2,)), dma((n // 2,)),
            dma((zs,)), dma((zs,)), dma((zs,)), dma((zs,)),
        ],
        compiler_params=pltpu.CompilerParams(
            collective_id=0, has_side_effects=True, vmem_limit_bytes=52 * 2**20
        ),
    )(pair_allowed, queries, key_rows, value_rows, out_grad, out_weight)


def solution(mesh):
    both = P(("groups", "ctx"), None)
    return jax.shard_map(
        functools.partial(per_device, mesh.shape["ctx"]),
        mesh=mesh,
        in_specs=(both, both, both, both, P("ctx", None), P("groups", None)),
        out_specs=(both,) * 5,
        check_vma=False,
    )
```

time: 188 us -> 96.4 us (0.51); the launches traced: 186 us -> 96.1 us
  waiting for transfers between devices: 96 us -> 0 us
  Pallas kernels: 0 us -> 87.8 us
  local copies, waits for them, and re-layouts: 32.9 us -> 7.62 us
  matrix products: 19.9 us -> 0 us
  between operations: 14.4 us -> 0.64 us
  other arithmetic: 12.7 us -> 0 us
  starting transfers between devices: 9.76 us -> 0 us
    pallas_call x0 -> x1, Pallas kernels: none -> 87.8 us  [per_device(): pl.pallas_call(functools.partial(kernel, n), out_shape=(jax.ShapeDtypeStr...]
    reduce_scatter x1 -> x0, waiting for transfers between devices: 40.4 us -> none  [per_device(): lax.psum_scatter(lax.dot_general(columns, attn, (((0,), (0,)), ((), ())),...]
    ppermute x4 -> x0, waiting for transfers between devices: 37.6 us -> none  [shifted(): return lax.ppermute(block, axis, route)]
    dot_general x9 -> x0, matrix products: 19.9 us -> none  [the longest x1 5.55 us: per_device(): lax.dot_general(columns, attn, (((0,), (0,)), ((), ())), preferred_elemen...]
    all_gather x1 -> x0, waiting for transfers between devices: 17.3 us -> none  [per_device(): lax.all_gather(out_weight, 'ctx', axis=0, tiled=True)]
    ppermute x4 -> x0, starting transfers between devices: 9.68 us -> none  [shifted(): return lax.ppermute(block, axis, route)]
    reshape x4 -> x0, local copies, waits for them, and re-layouts: 9.44 us -> none  [the longest x1 3.14 us: per_device(): value_part = value_part.reshape(count, SPAN + 1, BLK, feature_width)]
    transpose x2 -> x0, local copies, waits for them, and re-layouts: 5.83 us -> none  [the longest x1 3.47 us: per_device(): jnp.einsum('ahqk,aqhd->akhd', score_grad, query_heads, preferred_element_...]
  transfers between devices with their start and end apart: 6 -> 0, of which waited for: 6 -> 0; matrix products, arithmetic and copies ran while one was open for 33% -> 0% of each run, Pallas kernels for 0% -> 0%
where the time goes in v1:
time: 96.4 us; the launch traced here: 96.1 us
  Pallas kernels  87.8 us (91%)
  local copies, waits for them, and re-layouts  7.62 us (8%)
    pallas_call x1, Pallas kernels, per_device(): pl.pallas_call(functools.partial(kernel, n), out_shape=(jax.ShapeDtypeStr...  87.8 us
    unnamed x10, local copies, waits for them, and re-layouts  7.62 us

profile of v1, /device:TPU:8, one launch (start us, length us, event | category | flops | bytes accessed | tf_op | source)
XLA Modules:
  0.0 96.1 jit_solution(14337807179685124951)
XLA Ops:
  0.6 0.8 copy.11.pa
  1.4 0.0 copy-start
  1.4 0.9 copy-done
  2.3 87.8 %shard_map.101 = (bf16[256,2048]{1,0:T(8,128)(2,1)}, bf16[256,1024]{1,0:T(8,128)(2,1)S(1)}, bf16[256,1024]{1,0:T(8,128)(2,1)S(1)}, bf16[256,1024]{1,0:T(8,128)(2,1)S(1)}, f32[128,1024]{1,0:T(8,128)}) custom-call(s32[32,2]{1,0:T(8,128)S(1)} %copy.11.pa, bf16[256,1024]{1,0:T(8,128)(2,1)} %q.1, bf16[256,1024]{1,0:T(8,128)(2,1)} %k.1, bf16[256,1024]{1,0:T(8,128)(2,1)} %v.1, ...), custom_call_target="tpu_custom_call" | custom-call | tf_op jit(solution)/shard_map/pallas_call | solution.py:352
  90.2 2.3 %copy.17 = bf16[256,2048]{1,0:T(8,128)(2,1)} copy(bf16[256,2048]{1,0:T(8,128)(2,1)} %get-tuple-element.10) | data formatting | bytes 2097152
  92.5 0.8 copy.18
  93.3 0.8 copy.19
  94.1 0.0 copy-start.1
  94.1 0.8 copy.20
  94.9 0.4 copy-done.1
  95.3 0.8 copy.21
Async XLA Ops:
  1.4 0.9 copy-start
  94.1 1.2 %copy-start.1 = (f32[128,1024]{1,0:T(8,128)S(1)}, f32[128,1024]{1,0:T(8,128)}, u32[]{:S(2)}) copy-start(f32[128,1024]{1,0:T(8,128)} %get-tuple-element.14) | copy-start | bytes 1572868

commit v2 on v1

--- a/solution.py
+++ b/solution.py
@@ -98,7 +98,6 @@
         return c
 
     lax.fori_loop(1, zs, start_z, 0)
-    w_copy(0, hm, me, ypeer).start()
     w_copy(2, 0, me, sib).start()
     w_copy(2, 1, me, sib).start()
 
@@ -126,8 +125,6 @@
         w_copy(2, hm, idx, sib).start()
         return c
 
-    lax.fori_loop(1, zs, from_z, 0)
-
     @pl.when(me == 0)
     def _():
         k_halo[...] = jnp.zeros_like(k_halo)
@@ -137,6 +134,29 @@
         at = pl.ds(pl.multiple_of(j * HD, HD), HD)
         own = pl.ds(pl.multiple_of(i * half + j * HD, HD), HD)
         return jnp.concatenate([halo_ref[i, :, at], ref[:, own]], axis=0), own
+
+    def from_y(step, c):
+        idx = index(lax.rem(z + step, zs), 1 - y, core)
+        w_copy(0, hm, idx, xpeer).wait_recv()
+        w_copy(1, hm, idx, xpeer).start()
+        w_copy(2, hm, idx, sib).start()
+        return c
+
+    def from_x(yy):
+        def go(step, c):
+            idx = index(lax.rem(z + step, zs), yy, core)
+            w_copy(1, ho, idx, xpeer).wait_recv()
+            w_copy(2, ho, idx, sib).start()
+            return c
+
+        return go
+
+    def from_sib(h):
+        def go(o, c):
+            w_copy(2, h, o * 2 + 1 - core, sib).wait_recv()
+            return c
+
+        return go
 
     for i in range(2):
         @pl.when(me > 0)
@@ -157,6 +177,11 @@
             return c
 
         lax.fori_loop(0, H // 2, forward, 0)
+        if i == 0:
+            w_copy(0, hm, me, ypeer).start()
+            lax.fori_loop(1, zs, from_z, 0)
+        else:
+            lax.fori_loop(1, zs, from_x(y), 0)
 
     def c_copy(o):
         return rc(part.at[o * 2 + 1 - core], from_core.at[o], c_send.at[o], c_recv.at[o], sib)
@@ -168,6 +193,7 @@
         part[pl.ds(j * per_chunk, per_chunk)] = r.reshape(per_chunk, depth, 2 * half)
         for b in range(per_chunk // 2):
             c_copy(j * (per_chunk // 2) + b).start()
+        lax.fori_loop((t * zs) // chunks, ((t + 1) * zs) // chunks, from_y, 0)
         return c
 
     lax.fori_loop(0, chunks, share, 0)
@@ -185,50 +211,19 @@
 
     lax.fori_loop(1, zs + 1, stage_y, 0)
 
-    def from_y(step, c):
-        idx = index(lax.rem(z + step, zs), 1 - y, core)
-        w_copy(0, hm, idx, xpeer).wait_recv()
-        w_copy(1, hm, idx, xpeer).start()
-        w_copy(2, hm, idx, sib).start()
-        return c
-
-    lax.fori_loop(0, zs, from_y, 0)
-
-    def from_x(step, c):
-        for yy in range(2):
-            idx = index(lax.rem(z + step, zs), (y, 1 - y)[yy], core)
-
-            def go(idx=idx):
-                w_copy(1, ho, idx, xpeer).wait_recv()
-                w_copy(2, ho, idx, sib).start()
-
-            if yy == 0:
-                pl.when(step > 0)(go)
-            else:
-                go()
-        return c
-
-    lax.fori_loop(0, zs, from_x, 0)
-
-    def from_sib(o, c):
-        for h in range(2):
-            w_copy(2, h, o * 2 + 1 - core, sib).wait_recv()
-        return c
-
-    lax.fori_loop(0, n // 2, from_sib, 0)
-
-    for h in range(2):
+    def attn_grad(h):
         for part_of in range(half // CHUNK):
             cols = slice(part_of * CHUNK, (part_of + 1) * CHUNK)
             r = dot(og[...], wbuf[h, :, :, cols].reshape(n * depth, CHUNK), 1, 0)
-            da[:, h * half + part_of * CHUNK:h * half + (part_of + 1) * CHUNK] = r.astype(BF16)
+            at = pl.ds(pl.multiple_of(h * half + part_of * CHUNK, CHUNK), CHUNK)
+            da[:, at] = r.astype(BF16)
 
     def back_copy(i, part_of):
         src, dst = ((dk_out, dk_in), (dv_out, dv_in))[part_of]
         at = 2 * i + part_of
         return rc(src.at[i], dst.at[i], back_send.at[at], back_recv.at[at], down)
 
-    for i in range(2):
+    def backward_half(i):
         def backward(j, c):
             keys, own = ext(k, k_halo, i, j)
             values, _ = ext(v, v_halo, i, j)
@@ -268,7 +263,16 @@
         z_copy(zz, z).start()
         return c
 
-    lax.fori_loop(1, zs, stage_z, 0)
+    early = 1 + zs // 2
+    lax.fori_loop(0, n // 2, from_sib(hm), 0)
+    attn_grad(hm)
+    backward_half(hm)
+    lax.fori_loop(1, early, stage_z, 0)
+    lax.fori_loop(0, zs, from_x(1 - y), 0)
+    lax.fori_loop(0, n // 2, from_sib(ho), 0)
+    attn_grad(ho)
+    backward_half(ho)
+    lax.fori_loop(early, zs, stage_z, 0)
 
     def layer(j, c):
         rows_of = pl.ds(j * per_chunk, per_chunk)

time: 96.4 us -> 90.2 us (0.936)
  Pallas kernels: 87.8 us -> 81.6 us
    pallas_call x1, Pallas kernels: 87.8 us -> 81.6 us  [per_device(): pl.pallas_call(functools.partial(kernel, n), out_shape=(jax.ShapeDtypeStr...]
where the time goes in v2:
time: 90.2 us; the launch traced here: 89.9 us
  Pallas kernels  81.6 us (90%)
  local copies, waits for them, and re-layouts  7.62 us (8%)
    pallas_call x1, Pallas kernels, per_device(): pl.pallas_call(functools.partial(kernel, n), out_shape=(jax.ShapeDtypeStr...  81.6 us
    unnamed x10, local copies, waits for them, and re-layouts  7.62 us

profile of v2, /device:TPU:8, one launch (start us, length us, event | category | flops | bytes accessed | tf_op | source)
XLA Modules:
  0.0 89.9 jit_solution(13098698469355166781)
XLA Ops:
  0.6 0.8 copy.11.pa
  1.4 0.0 copy-start
  1.4 0.9 %copy-done = bf16[128,1024]{1,0:T(8,128)(2,1)S(1)} copy-done((bf16[128,1024]{1,0:T(8,128)(2,1)S(1)}, bf16[128,1024]{1,0:T(8,128)(2,1)}, u32[]{:S(2)}) %copy-start) | copy-done | bytes 262168
  2.3 81.6 %shard_map.101 = (bf16[256,2048]{1,0:T(8,128)(2,1)}, bf16[256,1024]{1,0:T(8,128)(2,1)S(1)}, bf16[256,1024]{1,0:T(8,128)(2,1)S(1)}, bf16[256,1024]{1,0:T(8,128)(2,1)S(1)}, f32[128,1024]{1,0:T(8,128)}) custom-call(s32[32,2]{1,0:T(8,128)S(1)} %copy.11.pa, bf16[256,1024]{1,0:T(8,128)(2,1)} %q.1, bf16[256,1024]{1,0:T(8,128)(2,1)} %k.1, bf16[256,1024]{1,0:T(8,128)(2,1)} %v.1, ...), custom_call_target="tpu_custom_call" | custom-call | tf_op jit(solution)/shard_map/pallas_call | solution.py:356
  84.0 2.3 %copy.17 = bf16[256,2048]{1,0:T(8,128)(2,1)} copy(bf16[256,2048]{1,0:T(8,128)(2,1)} %get-tuple-element.10) | data formatting | bytes 2097152
  86.3 0.8 copy.18
  87.1 0.8 copy.19
  87.9 0.0 copy-start.1
  87.9 0.8 copy.20
  88.7 0.4 copy-done.1
  89.1 0.8 copy.21
Async XLA Ops:
  1.4 0.9 %copy-start = (bf16[128,1024]{1,0:T(8,128)(2,1)S(1)}, bf16[128,1024]{1,0:T(8,128)(2,1)}, u32[]{:S(2)}) copy-start(bf16[128,1024]{1,0:T(8,128)(2,1)} %w.1) | copy-start | bytes 786436
  87.9 1.2 %copy-start.1 = (f32[128,1024]{1,0:T(8,128)S(1)}, f32[128,1024]{1,0:T(8,128)}, u32[]{:S(2)}) copy-start(f32[128,1024]{1,0:T(8,128)} %get-tuple-element.14) | copy-start | bytes 1572868

commit v3 on v2

--- a/solution.py
+++ b/solution.py
@@ -98,6 +98,7 @@
         return c
 
     lax.fori_loop(1, zs, start_z, 0)
+    w_copy(0, hm, me, ypeer).start()
     w_copy(2, 0, me, sib).start()
     w_copy(2, 1, me, sib).start()
 
@@ -178,7 +179,6 @@
 
         lax.fori_loop(0, H // 2, forward, 0)
         if i == 0:
-            w_copy(0, hm, me, ypeer).start()
             lax.fori_loop(1, zs, from_z, 0)
         else:
             lax.fori_loop(1, zs, from_x(y), 0)

time: 90.2 us -> 90 us (level)
  no operation moved by 1% of the time
where the time goes in v3:
time: 90 us; the launch traced here: 89.7 us
  Pallas kernels  81.4 us (90%)
  local copies, waits for them, and re-layouts  7.62 us (8%)
    pallas_call x1, Pallas kernels, per_device(): pl.pallas_call(functools.partial(kernel, n), out_shape=(jax.ShapeDtypeStr...  81.4 us
    unnamed x10, local copies, waits for them, and re-layouts  7.62 us

profile of v3, /device:TPU:8, one launch (start us, length us, event | category | flops | bytes accessed | tf_op | source)
XLA Modules:
  0.0 89.7 jit_solution(5493676017954528026)
XLA Ops:
  0.6 0.8 copy.11.pa
  1.4 0.0 copy-start
  1.4 0.9 %copy-done = bf16[128,1024]{1,0:T(8,128)(2,1)S(1)} copy-done((bf16[128,1024]{1,0:T(8,128)(2,1)S(1)}, bf16[128,1024]{1,0:T(8,128)(2,1)}, u32[]{:S(2)}) %copy-start) | copy-done | bytes 262168
  2.3 81.4 %shard_map.101 = (bf16[256,2048]{1,0:T(8,128)(2,1)}, bf16[256,1024]{1,0:T(8,128)(2,1)S(1)}, bf16[256,1024]{1,0:T(8,128)(2,1)S(1)}, bf16[256,1024]{1,0:T(8,128)(2,1)S(1)}, f32[128,1024]{1,0:T(8,128)}) custom-call(s32[32,2]{1,0:T(8,128)S(1)} %copy.11.pa, bf16[256,1024]{1,0:T(8,128)(2,1)} %q.1, bf16[256,1024]{1,0:T(8,128)(2,1)} %k.1, bf16[256,1024]{1,0:T(8,128)(2,1)} %v.1, ...), custom_call_target="tpu_custom_call" | custom-call | tf_op jit(solution)/shard_map/pallas_call | solution.py:356
  83.8 2.3 %copy.17 = bf16[256,2048]{1,0:T(8,128)(2,1)} copy(bf16[256,2048]{1,0:T(8,128)(2,1)} %get-tuple-element.10) | data formatting | bytes 2097152
  86.1 0.8 copy.18
  86.9 0.8 copy.19
  87.7 0.0 copy-start.1
  87.7 0.8 copy.20
  88.5 0.4 copy-done.1
  88.9 0.8 copy.21
Async XLA Ops:
  1.4 0.9 %copy-start = (bf16[128,1024]{1,0:T(8,128)(2,1)S(1)}, bf16[128,1024]{1,0:T(8,128)(2,1)}, u32[]{:S(2)}) copy-start(bf16[128,1024]{1,0:T(8,128)(2,1)} %w.1) | copy-start | bytes 786436
  87.7 1.2 %copy-start.1 = (f32[128,1024]{1,0:T(8,128)S(1)}, f32[128,1024]{1,0:T(8,128)}, u32[]{:S(2)}) copy-start(f32[128,1024]{1,0:T(8,128)} %get-tuple-element.14) | copy-start | bytes 1572868
